TPU v7x, 128 devices: a whole 4x4x4 slice. The times are simulated.
128 devices in a mesh: pipe: 8 (over x, core), mp: 16 (over y, z).
Axes of the slice: x: 4, y: 4, z: 4, core: 2. Of those that a mesh axis runs over, the one named last changes fastest.
Arguments:
- inbox: bfloat16 [8, 2048, 4096], P('pipe', 'mp'), may hold values from -45 to 45
- norm_gain: float32 [8, 4096], P('pipe'), may hold values from 0.5 to 1.5
- w_in: bfloat16 [8, 4096, 3, 6144], P('pipe', None, None, 'mp'), may hold values from -0.09375 to 0.09375
- short_w: float32 [8, 7, 3, 6144], P('pipe', None, None, 'mp'), may hold values from -2 to 2
- long_h: bfloat16 [8, 128, 6144], P('pipe', None, 'mp'), may hold values from -0.5 to 0.5
- skip_gain: float32 [8, 6144], P('pipe', 'mp'), may hold values from -1 to 1
- w_out: bfloat16 [8, 6144, 4096], P('pipe', 'mp'), may hold values from -0.078125 to 0.078125
Outputs:
- next_inbox: bfloat16 [8, 2048, 4096], P('pipe', 'mp')
All inputs are finite; a program needn't handle non-finite values.
Results may differ from a plain program's by a relative error of at most 0.015.
Values may be sent and summed in bfloat16 or wider, within the bound.
A program may use at most 320 MiB of HBM per device.

v0:
```python
import math

import jax
import jax.numpy as jnp
from jax import lax
from jax.sharding import PartitionSpec as P

FILT = 128
KSHORT = 7
LENGTH = 1024
SEQS = 2


def from_behind(block, axis, distance):
    devices = range(lax.axis_size(axis))
    route = [((i - distance) % len(devices), i) for i in devices]
    return lax.ppermute(block, axis, route)


def normalize(rows, gain):
    rows_f = rows.astype(jnp.float32)
    scale = lax.rsqrt(jnp.mean(rows_f * rows_f, axis=-1, keepdims=True) + 1e-06)
    return (rows_f * scale * gain).astype(jnp.bfloat16)


def band_table(taps, block_rows):
    chans = taps.shape[1]
    span = FILT + block_rows
    lead = jnp.zeros((1, chans), taps.dtype)
    tail = jnp.zeros((block_rows, chans), taps.dtype)
    line = jnp.concatenate([lead, taps[::-1], tail], axis=0)
    tiled = jnp.tile(line, (block_rows, 1))[: block_rows * span]
    return tiled.reshape(block_rows, span, chans)


def filter_rows(padded_u, taps, start, count):
    chans = padded_u.shape[1]
    block_rows = math.gcd(count, FILT)
    nblocks = count // block_rows
    ahead = FILT // block_rows
    pieces = padded_u.reshape(nblocks + ahead, block_rows, chans)
    windows = jnp.concatenate([pieces[k : k + nblocks] for k in range(ahead + 1)], axis=1)
    first = start + jnp.arange(nblocks, dtype=jnp.int32) * block_rows
    seq_start = first // LENGTH * LENGTH
    global_row = first[:, None] - FILT + jnp.arange(FILT + block_rows, dtype=jnp.int32)[None, :]
    inside = global_row >= seq_start[:, None]
    windows = jnp.where(inside[:, :, None], windows, jnp.zeros_like(windows))
    toeplitz = band_table(taps, block_rows)
    result = jnp.einsum("twc,bwc->btc", toeplitz, windows, preferred_element_type=jnp.float32)
    return result.reshape(count, chans)


def on_device(inbox, norm_gain, w_in, short_w, long_h, skip_gain, w_out):
    rows = inbox[0]
    gain = norm_gain[0]
    chans = w_in.shape[3]
    width_in = w_in.shape[1]
    w_proj = w_in[0].reshape(width_in, 3 * chans)
    proj = jnp.dot(
        lax.all_gather(normalize(rows, gain), "mp", axis=0, tiled=True),
        w_proj,
        preferred_element_type=jnp.float32,
    )
    proj = proj.astype(jnp.bfloat16).reshape(SEQS, LENGTH, 3 * chans).astype(jnp.float32)
    padded = jnp.pad(proj, ((0, 0), (KSHORT - 1, 0), (0, 0)))
    short_flat = short_w[0].reshape(KSHORT, 3 * chans)
    featured = jnp.zeros((SEQS, LENGTH, 3 * chans), jnp.float32)
    for j in range(KSHORT):
        featured = featured + short_flat[j] * padded[:, KSHORT - 1 - j : KSHORT - 1 - j + LENGTH]
    total_rows = SEQS * LENGTH
    query = featured[:, :, :chans].reshape(total_rows, chans)
    keys = featured[:, :, chans : 2 * chans]
    values = featured[:, :, 2 * chans :]
    mixed_kv = (keys * values).astype(jnp.bfloat16).reshape(total_rows, chans)
    padded_u = jnp.concatenate([jnp.zeros((FILT, chans), jnp.bfloat16), mixed_kv], axis=0)
    taps = long_h[0]
    skip = skip_gain[0]
    w_back = w_out[0]
    filtered = filter_rows(padded_u, taps, 0, total_rows)
    u_rows = mixed_kv.astype(jnp.float32)
    gated = (query * (filtered + skip * u_rows)).astype(jnp.bfloat16)
    mixed = lax.psum_scatter(
        jnp.dot(gated, w_back, preferred_element_type=jnp.float32).astype(jnp.bfloat16),
        "mp",
        scatter_dimension=0,
        tiled=True,
    ).astype(jnp.float32)
    result = (rows.astype(jnp.float32) + mixed).astype(jnp.bfloat16)
    moved = from_behind(result, "pipe", 1)
    return moved[None]


def solution(mesh):
    return jax.shard_map(
        on_device,
        mesh=mesh,
        in_specs=(
            P("pipe", "mp", None),
            P("pipe", None),
            P("pipe", None, None, "mp"),
            P("pipe", None, None, "mp"),
            P("pipe", None, "mp"),
            P("pipe", "mp"),
            P("pipe", "mp", None),
        ),
        out_specs=P("pipe", "mp", None),
        check_vma=False,
    )
```

profile of v0, /device:TPU:0, one launch (start us, length us, event | category | flops | bytes accessed | tf_op | source)
XLA Modules:
  0.0 366.5 jit_solution(12133267666712543093)
XLA Ops:
  6.5 1.7 fusion.7
  8.2 2.5 fusion.9
  10.8 12.5 %copy.12 = bf16[1,4096,3,384]{1,3,2,0:T(8,128)(2,1)} copy(bf16[1,4096,3,384]{3,1,2,0:T(8,128)(2,1)} %param.9) | data formatting | bytes 18874368 | tf_op args[2]
  23.9 8.9 %tile.4 = bf16[128,257,384]{2,1,0:T(8,128)(2,1)} broadcast(bf16[257,384]{1,0:T(8,128)(2,1)S(1)} %maximum_maximum_fusion), dimensions={1,2} | broadcast | bytes 25461504 | tf_op jit(solution)/shard_map/tile | solution.py:32
  32.8 25.5 %tile.10 = bf16[32896,384]{1,0:T(8,128)(2,1)} reshape(bf16[128,257,384]{2,1,0:T(8,128)(2,1)} %tile.4) | data formatting | bytes 50528256 | tf_op jit(solution)/shard_map/tile | solution.py:32
  58.3 20.6 %slice.92 = bf16[32768,384]{1,0:T(8,128)(2,1)} slice(bf16[32896,384]{1,0:T(8,128)(2,1)} %tile.10), slice={[0:32768], [0:384]} | slice | bytes 50331648 | tf_op jit(solution)/shard_map/slice | solution.py:32
  78.9 32.5 %copy.18 = bf16[128,256,384]{1,0,2:T(8,128)(2,1)} copy(bf16[128,256,384]{2,1,0:T(8,128)(2,1)} %bitcast.35) | data formatting | bytes 50331648 | tf_op jit(solution)/shard_map/reshape | solution.py:33
  111.5 13.4 %all-gather.2.cloned.1.call-done = bf16[2048,4096]{1,0:T(8,128)(2,1)} async-done(((bf16[128,4096]{1,0:T(8,128)(2,1)}), bf16[2048,4096]{1,0:T(8,128)(2,1)}) %all-gather.2.cloned.1.call-update) | async-done | bytes 16777232 | tf_op jit(solution)/shard_map/all_gather | solution.py:60
  124.9 27.4 %convolution_convert_fusion.1 = bf16[2048,1152]{1,0:T(8,128)(2,1)S(1)} fusion(bf16[2048,4096]{1,0:T(8,128)(2,1)} %all-gather.2.cloned.1.call-done, bf16[4096,1152]{0,1:T(8,128)(2,1)} %bitcast.39), kind=kOutput, calls=%fused_computation.2 | convolution fusion | flops 19329712128 | bytes 30932992 | tf_op jit(solution)/shard_map/dot_general | solution.py:59
  152.3 4.3 %convert.3 = f32[2,1024,1152]{2,1,0:T(8,128)} convert(bf16[2,1024,1152]{2,1,0:T(8,128)(2,1)S(1)} %bitcast.41) | non-fusion elementwise | flops 2359296 | bytes 14155776 | tf_op jit(solution)/shard_map/convert_element_type | solution.py:64
  156.6 27.0 %multiply_add_fusion = f32[2,1024,1152]{2,1,0:T(8,128)} fusion(f32[2,1024,1152]{2,1,0:T(8,128)} %convert.3, f32[1152]{0:T(1024)S(1)} %mul.150, f32[1152]{0:T(1024)S(1)} %mul.147, f32[1152]{0:T(1024)S(1)} %mul.144, f32[1152]{0:T(1024)S(1)} %mul.141, f32[1152]{0:T(1024)S(1)} %mul.138, f32[1152]{0:T(1024)S(1)} %mul.135, f32[1152]{0:T(1024)S(1)} %mul.126), kind=kLoop, calls=%fused_computation.1 | loop fusion | flops 30670848 | bytes 18906624 | tf_op jit(solution)/shard_map/add | solution.py:69
  183.6 4.3 %fusion = bf16[2,1024,384]{2,1,0:T(8,128)(2,1)} fusion(f32[2,1024,1152]{2,1,0:T(8,128)} %multiply_add_fusion), kind=kLoop, calls=%fused_computation.4 | loop fusion | flops 1572864 | bytes 7864320 | tf_op jit(solution)/shard_map/convert_element_type | solution.py:74
  187.9 3.0 copy.17
  190.9 2.7 copy.13
  193.5 1.6 fusion.12
  195.1 1.6 copy.20
  196.7 13.7 %fusion.11 = f32[16,128,384]{1,0,2:T(8,128)} fusion(bf16[128,256,384]{1,0,2:T(8,128)(2,1)} %copy.18, bf16[16,128,384]{1,0,2:T(8,128)(2,1)} %copy.17, bf16[16,128,384]{1,0,2:T(8,128)(2,1)} %bitcast.40, pred[16,256]{1,0:T(8,128)(4,1)S(1)} %add_compare_fusion), kind=kOutput, calls=%fused_computation.21 | convolution fusion | flops 410517504 | bytes 31461376 | tf_op jit(solution)/shard_map/twc,bwc->btc/dot_general | solution.py:49
  210.3 3.5 copy.19
  213.9 5.3 %fusion.1 = bf16[2,1024,384]{2,1,0:T(8,128)(2,1)S(1)} fusion(f32[2,1024,1152]{2,1,0:T(8,128)} %multiply_add_fusion, f32[384]{0:T(512)S(1)} %reduce.7, f32[2,1024,384]{2,1,0:T(8,128)} %bitcast.38), kind=kLoop, calls=%fused_computation.6 | loop fusion | flops 5505024 | bytes 14157312 | tf_op jit(solution)/shard_map/convert_element_type | solution.py:81
  219.2 11.7 %convolution_convert_fusion = bf16[2048,4096]{1,0:T(8,128)(2,1)} fusion(bf16[2048,384]{1,0:T(8,128)(2,1)S(1)} %bitcast.42, bf16[1,384,4096]{2,1,0:T(8,128)(2,1)S(1)} %copy-done), kind=kOutput, calls=%fused_computation | convolution fusion | flops 6450839552 | bytes 21495808 | tf_op jit(solution)/shard_map/dot_general | solution.py:83
  231.0 110.5 %reduce-scatter.2.cloned.1.call-done = bf16[128,4096]{1,0:T(8,128)(2,1)} async-done(((bf16[2048,4096]{1,0:T(8,128)(2,1)}), bf16[128,4096]{1,0:T(8,128)(2,1)}) %reduce-scatter.2.cloned.1.call-update) | async-done | bytes 1048592 | tf_op jit(solution)/shard_map/reduce_scatter | solution.py:82
  341.5 1.8 fusion.10
  343.3 15.4 %collective-permute-done = bf16[128,4096]{1,0:T(8,128)(2,1)S(1)} collective-permute-done((bf16[128,4096]{1,0:T(8,128)(2,1)S(1)}, bf16[128,4096]{1,0:T(8,128)(2,1)S(1)}, u32[]{:S(2)}, u32[]{:S(2)}) %collective-permute-start) | collective-permute-done | bytes 1048608 | tf_op jit(solution)/shard_map/ppermute | solution.py:17
  358.7 1.0 copy.22
  (30 shorter events, 0.8 us)
Async XLA Ops:
  6.5 212.7 %copy-start = (bf16[1,384,4096]{2,1,0:T(8,128)(2,1)S(1)}, bf16[1,384,4096]{2,1,0:T(8,128)(2,1)}, u32[]{:S(2)}) copy-start(bf16[1,384,4096]{2,1,0:T(8,128)(2,1)} %param.13) | copy-start | bytes 9437188
  6.5 118.3 %all-gather.2.cloned.1.call-start = ((), (), s32[]{:S(2)}) async-start(), calls=%async_computation.1 | async-start | bytes 17825792 | tf_op jit(solution)/shard_map/all_gather | solution.py:60
  10.8 12.6 %copy-start.2 = (f32[1,7,3,384]{3,0,2,1:T(1,128)S(1)}, f32[1,7,3,384]{3,0,2,1:T(1,128)}, u32[]{:S(2)}) copy-start(f32[1,7,3,384]{3,0,2,1:T(1,128)} %param.10) | copy-start | bytes 96772
  10.8 12.7 %copy-start.1 = (bf16[1,128,384]{2,1,0:T(8,128)(2,1)S(1)}, bf16[1,128,384]{2,1,0:T(8,128)(2,1)}, u32[]{:S(2)}) copy-start(bf16[1,128,384]{2,1,0:T(8,128)(2,1)} %param.11) | copy-start | bytes 294916
  10.8 330.7 %reduce-scatter.2.cloned.1.call-start = ((), (), s32[]{:S(2)}) async-start(), calls=%async_computation.2 | async-start | bytes 17825792 | tf_op jit(solution)/shard_map/reduce_scatter | solution.py:82
  78.9 32.5 %copy-start.3 = (f32[1,384]{1,0:T(1,128)S(1)}, f32[1,384]{1,0:T(1,128)}, u32[]{:S(2)}) copy-start(f32[1,384]{1,0:T(1,128)} %param.12) | copy-start | bytes 4612
  343.3 15.4 %collective-permute-start = (bf16[128,4096]{1,0:T(8,128)(2,1)S(1)}, bf16[128,4096]{1,0:T(8,128)(2,1)S(1)}, u32[]{:S(2)}, u32[]{:S(2)}) collective-permute-start(bf16[128,4096]{1,0:T(8,128)(2,1)S(1)} %fusion.10), channel_id=1, source_target_pairs={{112,0},{0,16},{16,32},{32,48},{48,64},{64,80},{80,96},{96,112},{1... | collective-permute-start | bytes 3145736 | tf_op jit(solution)/shard_map/ppermute | solution.py:17
Sparse Core Ops, SparseCore 0:
  10.9 113.9 all-gather.1
  231.1 110.3 reduce-scatter.1
where the time goes:
time: 368 us; the launch traced here: 367 us
  waiting for transfers between devices  139 us (38%)
  local copies, waits for them, and re-layouts  114 us (31%)
  matrix products  52.9 us (14%)
  other arithmetic  47.1 us (13%)
  between operations  13.5 us (4%)
    reduce_scatter x1, waiting for transfers between devices, on_device(): lax.psum_scatter(jnp.dot(gated, w_back, preferred_element_type=jnp.float3...  110 us
    another operation x2, local copies, waits for them, and re-layouts, band_table(): tiled = jnp.tile(line, (block_rows, 1))[:block_rows * span]  34.4 us
    reshape x1, local copies, waits for them, and re-layouts, band_table(): return tiled.reshape(block_rows, span, chans)  32.5 us
    dot_general x1, matrix products, on_device(): jnp.dot(lax.all_gather(normalize(rows, gain), 'mp', axis=0, tiled=True),...  27.4 us
    add x1, other arithmetic, on_device(): featured + short_flat[j] * padded[:, KSHORT - 1 - j:KSHORT - 1 - j + LENGTH]  27 us
    slice x1, local copies, waits for them, and re-layouts, band_table(): tiled = jnp.tile(line, (block_rows, 1))[:block_rows * span]  20.6 us
    unnamed x12, local copies, waits for them, and re-layouts  16.6 us
    ppermute x1, waiting for transfers between devices, from_behind(): return lax.ppermute(block, axis, route)  15.4 us
  transfers between devices with their start and end apart: 3, of which 3 were waited for; matrix products, arithmetic and copies ran while one was open for 27% of the time, Pallas kernels for 0%

commit v1 on v0

v1 whole, which is shorter than its diff:
```python
import functools

import jax
import jax.numpy as jnp
from jax import lax
from jax.experimental import pallas as pl
from jax.experimental.pallas import tpu as pltpu
from jax.sharding import PartitionSpec as P

MESH = pl.DeviceIdType.MESH
F32 = jnp.float32
BF16 = jnp.bfloat16

ROWS = 128
DW = 4096
CHANS = 384
FILT = 128
KSHORT = 7
SIDE = 4
SEQ_CHUNKS = 8
GATHER_A = 2048
REDUCE_A = 2048
LANES = 128

TOP = (0, ROWS // 2)
BOTTOM = (ROWS // 2, ROWS // 2)
FULL = (0, ROWS)


def message_names():
    names = []
    for group in ["1A", "1B"] + [f"2A{j}" for j in range(4)] + [f"2B{j}" for j in range(4)]:
        names += [(group, kind) for kind in ("n1", "n3", "v1", "v3")]
    for group in [f"R1A{j}" for j in range(4)] + [f"R1B{j}" for j in range(4)] + ["R2A", "R2B"]:
        names += [(group, kind) for kind in ("f1", "f3", "m1", "m3")]
    names += [("pipe", "A"), ("pipe", "B")]
    return {name: index for index, name in enumerate(names)}


NAMES = message_names()


def kernel(
    inbox, gain, w_hbm, short_w, long_h, skip, wo_hbm, out,
    x, w, acc, wo, gated, land_fa, land_fb, land_ma, land_mb, land2_fa, land2_fb, land2_ma, land2_mb,
    win, win3, taps, send_sem, recv_sem, load_sem,
):
    p = lax.axis_index("pipe")
    m = lax.axis_index("mp")
    sections = lax.axis_size("pipe")
    y, z = m // SIDE, m % SIDE
    ys = [y, y + 1 - 2 * (y % 2), (y + 2) % SIDE, SIDE - 1 - y]
    zs = [z, z + 1 - 2 * (z % 2), (z + 2) % SIDE, SIDE - 1 - z]
    after = (p + 1) % sections
    before = (p + sections - 1) % sections

    def device(yy, zz):
        return (p, yy * SIDE + zz)

    neighbours = [device(ys[1], z), device(ys[3], z), device(y, zs[1]), device(y, zs[3]), (after, m), (before, m)]
    barrier = pltpu.get_barrier_semaphore()
    for neighbour in neighbours:
        pl.semaphore_signal(barrier, inc=1, device_id=neighbour, device_id_type=MESH)

    loads = [
        pltpu.make_async_copy(w_hbm.at[i], w.at[:, pl.ds(i * CHANS, CHANS)], load_sem.at[i]) for i in range(3)
    ] + [pltpu.make_async_copy(wo_hbm, wo, load_sem.at[3])]
    for load in loads:
        load.start()

    def region(yy, zz, rows, cols):
        return x.at[yy * SIDE + zz, pl.ds(*rows), pl.ds(*cols)]

    def message(name, src, dst, dev):
        k = NAMES[name]
        return pltpu.make_async_remote_copy(
            src_ref=src, dst_ref=dst, send_sem=send_sem.at[k], recv_sem=recv_sem.at[k],
            device_id=dev, device_id_type=MESH,
        )

    class Ring:
        def __init__(self, group, dim, other, cols):
            self.group, self.dim, self.other, self.cols = group, dim, other, cols
            self.c = ys if dim == "y" else zs
            self.to1 = device(ys[1], z) if dim == "y" else device(y, zs[1])
            self.to3 = device(ys[3], z) if dim == "y" else device(y, zs[3])

        def at(self, k, rows):
            if self.dim == "y":
                return region(self.c[k], self.other, rows, self.cols)
            return region(self.other, self.c[k], rows, self.cols)

    class Gather(Ring):
        def msg(self, kind, k, rows, dev):
            return message((self.group, kind), self.at(k, rows), self.at(k, rows), dev)

        def send(self):
            self.msg("n1", 0, FULL, self.to1).start()
            self.msg("n3", 0, FULL, self.to3).start()

        def forward1(self):
            self.msg("n1", 1, FULL, self.to1).wait_recv()
            self.msg("v3", 1, TOP, self.to3).start()

        def forward3(self):
            self.msg("n3", 3, FULL, self.to3).wait_recv()
            self.msg("v1", 3, BOTTOM, self.to1).start()

        def far(self):
            self.msg("v3", 2, TOP, self.to3).wait_recv()
            self.msg("v1", 2, BOTTOM, self.to1).wait_recv()

        def sent(self):
            self.msg("n1", 0, FULL, self.to1).wait_send()
            self.msg("n3", 0, FULL, self.to3).wait_send()
            self.msg("v3", 1, TOP, self.to3).wait_send()
            self.msg("v1", 3, BOTTOM, self.to1).wait_send()

    class Reduce(Ring):
        def __init__(self, group, dim, other, cols, far, near):
            super().__init__(group, dim, other, cols)
            self.far, self.near = far, near

        def msg(self, kind):
            k, rows, land, dev = {
                "f3": (2, TOP, self.far.at[1], self.to3),
                "f1": (2, BOTTOM, self.far.at[0], self.to1),
                "m1": (1, FULL, self.near.at[0], self.to1),
                "m3": (3, FULL, self.near.at[1], self.to3),
            }[kind]
            return message((self.group, kind), self.at(k, rows), land, dev)

        def send_far(self):
            self.msg("f3").start()
            self.msg("f1").start()

        def merge1(self):
            self.msg("f3").wait_recv()
            here = self.at(1, TOP)
            here[...] = (here[...].astype(F32) + self.far[1].astype(F32)).astype(BF16)
            self.msg("m1").start()

        def merge3(self):
            self.msg("f1").wait_recv()
            here = self.at(3, BOTTOM)
            here[...] = (here[...].astype(F32) + self.far[0].astype(F32)).astype(BF16)
            self.msg("m3").start()

        def merge(self):
            self.merge1()
            self.merge3()

        def total(self, residual=None):
            self.msg("m1").wait_recv()
            self.msg("m3").wait_recv()
            here = self.at(0, FULL)

            def rows16(r, carry):
                rows = pl.ds(pl.multiple_of(r * 16, 16), 16)
                value = here[rows, :].astype(F32) + self.near[0, rows, :].astype(F32) + self.near[1, rows, :].astype(F32)
                if residual is not None:
                    value = value + inbox[rows, pl.ds(*self.cols)].astype(F32)
                here[rows, :] = value.astype(BF16)
                return carry

            lax.fori_loop(0, ROWS // 16, rows16, 0)

        def sent(self):
            for kind in ("f3", "f1", "m1", "m3"):
                self.msg(kind).wait_send()

    gather_a, gather_b = (0, GATHER_A), (GATHER_A, DW - GATHER_A)
    g1a = Gather("1A", "y", z, gather_a)
    g1b = Gather("1B", "z", y, gather_b)
    g2a = [Gather(f"2A{j}", "z", ys[j], gather_a) for j in range(4)]
    g2b = [Gather(f"2B{j}", "y", zs[j], gather_b) for j in range(4)]
    reduce_a, reduce_b = (0, REDUCE_A), (REDUCE_A, DW - REDUCE_A)
    r1a = [Reduce(f"R1A{j}", "z", ys[j], reduce_a, land_fa.at[j], land_ma.at[j]) for j in range(4)]
    r1b = [Reduce(f"R1B{j}", "y", zs[j], reduce_b, land_fb.at[j], land_mb.at[j]) for j in range(4)]
    r2a = Reduce("R2A", "y", z, reduce_a, land2_fa, land2_ma)
    r2b = Reduce("R2B", "z", y, reduce_b, land2_fb, land2_mb)

    def normalize(r, carry):
        rows = pl.ds(pl.multiple_of(r * 16, 16), 16)
        value = inbox[rows, :].astype(F32)
        scale = lax.rsqrt(jnp.mean(value * value, axis=-1, keepdims=True) + 1e-06)
        x[m, rows, :] = (value * scale * gain[...]).astype(BF16)
        return carry

    def project_a(first, zz):
        left = jnp.concatenate(
            [x[first + zz, :, pl.ds(*gather_a)], x[first + SIDE + zz, :, pl.ds(*gather_a)]], axis=0
        )
        part = jnp.dot(left, w[pl.ds(*gather_a), :], preferred_element_type=F32)
        acc[first + zz] += part[:ROWS]
        acc[first + SIDE + zz] += part[ROWS:]

    def project_b(yy):
        def two(k, carry):
            lo = yy * SIDE + 2 * k
            left = x[pl.ds(lo, 2), :, pl.ds(*gather_b)].reshape(2 * ROWS, gather_b[1])
            part = jnp.dot(left, w[pl.ds(*gather_b), :], preferred_element_type=F32)
            acc[lo] += part[:ROWS]
            acc[lo + 1] += part[ROWS:]
            return carry

        lax.fori_loop(0, 2, two, 0)

    def short_filter(first):
        def step(k, carry):
            i = SEQ_CHUNKS - 1 - k // 3
            lane = pl.multiple_of((k % 3) * LANES, LANES)
            chunk = first + i
            prev = jnp.maximum(chunk - 1, first)
            streams = []
            for s in range(3):
                cols = pl.ds(s * CHANS + lane, LANES)
                head = acc[prev, pl.ds(ROWS - 8, 8), cols].astype(BF16).astype(F32)
                win3[s, pl.ds(0, 8), :] = jnp.where(i > 0, head, jnp.zeros_like(head))
                win3[s, pl.ds(8, ROWS), :] = acc[chunk, :, cols].astype(BF16).astype(F32)
                value = short_w[pl.ds(0, 1), cols] * win3[s, pl.ds(8, ROWS), :]
                for j in range(1, KSHORT):
                    value = value + short_w[pl.ds(j, 1), cols] * win3[s, pl.ds(8 - j, ROWS), :]
                streams.append(value)
            acc[chunk, :, pl.ds(lane, LANES)] = streams[0]
            acc[chunk, :, pl.ds(CHANS + lane, LANES)] = (streams[1] * streams[2]).astype(BF16).astype(F32)
            return carry

        lax.fori_loop(0, SEQ_CHUNKS * 3, step, 0)

    def long_filter(first, start, count):
        def step(k, carry):
            i = start + k // 3
            lane = pl.multiple_of((k % 3) * LANES, LANES)
            chunk = first + i
            prev = jnp.maximum(chunk - 1, first)
            lanes = pl.ds(lane, LANES)
            u_cols = pl.ds(CHANS + lane, LANES)
            before_u = acc[prev, :, u_cols]
            win[pl.ds(0, ROWS), :] = jnp.where(i > 0, before_u, jnp.zeros_like(before_u))
            own_u = acc[chunk, :, u_cols]
            win[pl.ds(ROWS, ROWS), :] = own_u
            value = skip[:, lanes] * own_u
            for shift in range(8):
                shifted = win[pl.ds(8 - shift, 2 * ROWS - 8), :]
                for a in range(FILT // 8):
                    base = ROWS - 8 - 8 * a
                    value = value + taps[pl.ds(8 * a + shift, 1), lanes] * shifted[base : base + ROWS]
            gated[chunk, :, lanes] = (acc[chunk, :, lanes] * value).astype(BF16)
            return carry

        lax.fori_loop(0, count * 3, step, 0)

    def mix(yy, pair):
        lo = yy * SIDE + 2 * pair
        left = gated[pl.ds(lo, 2)].reshape(2 * ROWS, CHANS)

        def tile(n, carry):
            cols = pl.ds(pl.multiple_of(n * 1024, 1024), 1024)
            part = jnp.dot(left, wo[:, cols], preferred_element_type=F32).astype(BF16)
            x[lo, :, cols] = part[:ROWS]
            x[lo + 1, :, cols] = part[ROWS:]
            return carry

        lax.fori_loop(0, DW // 1024, tile, 0)

    lax.fori_loop(0, ROWS // 16, normalize, 0)
    pl.semaphore_wait(barrier, len(neighbours))
    g1a.send()
    g1b.send()
    g2a[0].send()
    g2b[0].send()

    def clear(k, carry):
        acc[k] = jnp.zeros((ROWS, 3 * CHANS), F32)
        return carry

    lax.fori_loop(0, SIDE * SIDE, clear, 0)
    taps[...] = long_h[...].astype(F32)
    for load in loads:
        load.wait()

    own = (y // 2) * SEQ_CHUNKS
    other = (1 - y // 2) * SEQ_CHUNKS

    g1a.forward1()
    g2a[1].send()
    g1a.forward3()
    g1b.forward1()
    g2b[1].send()
    g1b.forward3()
    g2b[3].send()
    g2a[0].forward1()
    g2a[0].forward3()
    g1b.far()
    g2b[2].send()
    project_b(y)
    g2a[1].forward1()
    g2a[1].forward3()
    g1a.far()
    g2a[2].send()
    g2a[3].send()
    g2b[0].forward1()
    g2b[0].forward3()
    project_a(other, z)
    g2b[1].forward1()
    g2b[1].forward3()
    g2a[0].far()
    g2a[1].far()
    lax.fori_loop(0, SIDE, lambda zz, c: (project_a(own, zz), c)[1], 0)
    g2b[3].forward1()
    g2b[3].forward3()
    g2a[2].forward1()
    g2a[2].forward3()
    g2b[2].forward1()
    g2b[2].forward3()
    project_b(ys[1])
    short_filter(own)
    long_filter(own, 0, 4)
    g2a[3].forward1()
    g2a[3].forward3()
    long_filter(own, 4, 4)
    project_b(ys[3])
    project_a(other, zs[1])
    project_a(other, zs[3])
    for ring in [g2a[2], g2a[3]] + g2b:
        ring.far()
    for ring in [g1a, g1b] + g2a + g2b:
        ring.sent()

    far_pair, near_pair = 1 - z // 2, z // 2
    mix(y, far_pair)
    r1a[0].send_far()
    mix(ys[1], far_pair)
    r1a[1].send_far()
    project_a(other, zs[2])
    project_b(ys[2])
    mix(y, near_pair)
    mix(ys[1], near_pair)
    r1a[0].merge()
    r1a[1].merge()
    short_filter(other)
    y2_at, y3_at = ys[2] * SIDE - other, ys[3] * SIDE - other
    long_filter(other, y2_at + 2 * far_pair, 2)
    mix(ys[2], far_pair)
    r1b[2].send_far()
    r1b[3].send_far()
    r1a[2].send_far()
    long_filter(other, y3_at + 2 * far_pair, 2)
    mix(ys[3], far_pair)
    r1a[3].send_far()
    long_filter(other, y2_at + 2 * near_pair, 2)
    mix(ys[2], near_pair)
    r1b[1].send_far()
    r1b[0].send_far()
    r1b[2].merge()
    r1b[3].merge()
    long_filter(other, y3_at + 2 * near_pair, 2)
    mix(ys[3], near_pair)
    r1a[2].merge()
    r1a[3].merge()
    r1b[1].merge()
    r1b[0].merge()
    r1a[0].total()
    r1a[1].total()
    r1b[2].total()
    r2b.send_far()
    r1b[3].total()
    r1a[2].total()
    r2a.send_far()
    r1a[3].total()
    r2b.merge3()
    r1b[1].total()
    r2b.merge1()
    r2a.merge1()
    r2a.merge3()
    r1b[0].total()
    r2b.total(inbox)
    hand_b = message(
        ("pipe", "B"), region(y, z, FULL, reduce_b), out.at[:, pl.ds(*reduce_b)], (after, m)
    )
    hand_b.start()
    r2a.total(inbox)
    hand_a = message(
        ("pipe", "A"), region(y, z, FULL, reduce_a), out.at[:, pl.ds(*reduce_a)], (after, m)
    )
    hand_a.start()
    for ring in r1a + r1b + [r2a, r2b]:
        ring.sent()
    hand_a.wait()
    hand_b.wait()


def on_device(inbox, norm_gain, w_in, short_w, long_h, skip_gain, w_out):
    vmem = pl.BlockSpec(memory_space=pltpu.VMEM)
    anywhere = pl.BlockSpec(memory_space=pl.ANY)
    count = len(NAMES)
    wide_a, wide_b = REDUCE_A, DW - REDUCE_A
    result = pl.pallas_call(
        kernel,
        out_shape=jax.ShapeDtypeStruct((ROWS, DW), BF16),
        in_specs=[vmem, vmem, anywhere, vmem, vmem, vmem, anywhere],
        out_specs=anywhere,
        scratch_shapes=[
            pltpu.VMEM((SIDE * SIDE, ROWS, DW), BF16),
            pltpu.VMEM((DW, 3 * CHANS), BF16),
            pltpu.VMEM((SIDE * SIDE, ROWS, 3 * CHANS), F32),
            pltpu.VMEM((CHANS, DW), BF16),
            pltpu.VMEM((SIDE * SIDE, ROWS, CHANS), BF16),
            pltpu.VMEM((4, 2, ROWS // 2, wide_a), BF16),
            pltpu.VMEM((4, 2, ROWS // 2, wide_b), BF16),
            pltpu.VMEM((4, 2, ROWS, wide_a), BF16),
            pltpu.VMEM((4, 2, ROWS, wide_b), BF16),
            pltpu.VMEM((2, ROWS // 2, wide_a), BF16),
            pltpu.VMEM((2, ROWS // 2, wide_b), BF16),
            pltpu.VMEM((2, ROWS, wide_a), BF16),
            pltpu.VMEM((2, ROWS, wide_b), BF16),
            pltpu.VMEM((2 * ROWS, LANES), F32),
            pltpu.VMEM((3, ROWS + 8, LANES), F32),
            pltpu.VMEM((FILT, CHANS), F32),
            pltpu.SemaphoreType.DMA((count,)),
            pltpu.SemaphoreType.DMA((count,)),
            pltpu.SemaphoreType.DMA((4,)),
        ],
        compiler_params=pltpu.CompilerParams(
            collective_id=0, has_side_effects=True, vmem_limit_bytes=62 * 1024 * 1024
        ),
        cost_estimate=pl.CostEstimate(flops=27_000_000_000, bytes_accessed=20_000_000, transcendentals=0),
        name="relay_block",
    )(
        inbox[0],
        norm_gain,
        jnp.transpose(w_in[0], (1, 0, 2)),
        short_w[0].reshape(KSHORT, 3 * CHANS),
        long_h[0],
        skip_gain,
        w_out[0],
    )
    return result[None]


def solution(mesh):
    return jax.shard_map(
        on_device,
        mesh=mesh,
        in_specs=(
            P("pipe", "mp", None),
            P("pipe", None),
            P("pipe", None, None, "mp"),
            P("pipe", None, None, "mp"),
            P("pipe", None, "mp"),
            P("pipe", "mp"),
            P("pipe", "mp", None),
        ),
        out_specs=P("pipe", "mp", None),
        check_vma=False,
    )
```

time: 368 us -> 215 us (0.58)
  Pallas kernels: 0 us -> 210 us
  waiting for transfers between devices: 139 us -> 0 us
  local copies, waits for them, and re-layouts: 114 us -> 2.91 us
  matrix products: 52.9 us -> 0 us
  other arithmetic: 47.1 us -> 0.84 us
  between operations: 13.5 us -> 0.01 us
    pallas_call x0 -> x1, Pallas kernels: none -> 210 us  [on_device(): pl.pallas_call(kernel, out_shape=jax.ShapeDtypeStruct((ROWS, DW), BF16),...]
    reduce_scatter x1 -> x0, waiting for transfers between devices: 110 us -> none  [on_device(): lax.psum_scatter(jnp.dot(gated, w_back, preferred_element_type=jnp.float3...]
    dot_general x3 -> x0, matrix products: 52.9 us -> none  [the longest x1 27.4 us: on_device(): jnp.dot(lax.all_gather(normalize(rows, gain), 'mp', axis=0, tiled=True),...]
    reshape x3 -> x0, local copies, waits for them, and re-layouts: 38.7 us -> none  [the longest x1 32.5 us: band_table(): return tiled.reshape(block_rows, span, chans)]
    another operation x3 -> x0, local copies, waits for them, and re-layouts: 34.4 us -> none  [the longest x2 34.4 us: band_table(): tiled = jnp.tile(line, (block_rows, 1))[:block_rows * span]]
    add x1 -> x0, other arithmetic: 27 us -> none  [on_device(): featured + short_flat[j] * padded[:, KSHORT - 1 - j:KSHORT - 1 - j + LENGTH]]
    slice x3 -> x0, local copies, waits for them, and re-layouts: 23.7 us -> none  [the longest x1 20.6 us: band_table(): tiled = jnp.tile(line, (block_rows, 1))[:block_rows * span]]
    convert_element_type x5 -> x0, other arithmetic: 18.2 us -> none  [the longest x1 5.3 us: on_device(): gated = (query * (filtered + skip * u_rows)).astype(jnp.bfloat16)]
  transfers between devices with their start and end apart: 3 -> 0, of which waited for: 3 -> 0; matrix products, arithmetic and copies ran while one was open for 27% -> 0% of each run, Pallas kernels for 0% -> 0%
where the time goes in v1:
time: 215 us; the launch traced here: 214 us
  Pallas kernels  210 us (98%)
  local copies, waits for them, and re-layouts  2.91 us (1%)
    pallas_call x1, Pallas kernels, on_device(): pl.pallas_call(kernel, out_shape=jax.ShapeDtypeStruct((ROWS, DW), BF16),...  210 us

profile of v1, /device:TPU:0, one launch (start us, length us, event | category | flops | bytes accessed | tf_op | source)
XLA Modules:
  0.0 213.9 jit_solution(5568386902127559724)
XLA Ops:
  0.0 0.8 reduce
  0.8 0.6 copy.8
  1.5 210.2 %relay_block.1 = bf16[128,4096]{1,0:T(8,128)(2,1)} custom-call(bf16[128,4096]{1,0:T(8,128)(2,1)} %bitcast.14, f32[1,4096]{1,0:T(1,128)} %gain.1, bf16[3,4096,384]{2,1,0:T(8,128)(2,1)} %bitcast.12, f32[7,1152]{1,0:T(8,128)} %bitcast.11, bf16[128,384]{1,0:T(8,128)(2,1)} %bitcast.15, f32[1,384]{1,0:T(1,128)} %skip.1, bf16[384,4096]{1,0:T(8,128)(2,1)} %bitcast.13), custom_call_target="tpu_custom_call" | custom-call | flops 27000000512 | bytes 20000000 | tf_op jit(solution)/shard_map/relay_block/pallas_call | solution.py:399
  211.7 2.3 %copy.10 = bf16[1,128,4096]{2,1,0:T(8,128)(2,1)} copy(bf16[1,128,4096]{2,1,0:T(8,128)(2,1)} %bitcast.9) | data formatting | bytes 2097152

commit v2 on v1

--- a/solution.py
+++ b/solution.py
@@ -18,9 +18,10 @@
 KSHORT = 7
 SIDE = 4
 SEQ_CHUNKS = 8
-GATHER_A = 2048
-REDUCE_A = 2048
+GATHER_A = 1792
+REDUCE_A = 2304
 LANES = 128
+PIECES = 2
 
 TOP = (0, ROWS // 2)
 BOTTOM = (ROWS // 2, ROWS // 2)
@@ -31,9 +32,9 @@
     names = []
     for group in ["1A", "1B"] + [f"2A{j}" for j in range(4)] + [f"2B{j}" for j in range(4)]:
         names += [(group, kind) for kind in ("n1", "n3", "v1", "v3")]
-    for group in [f"R1A{j}" for j in range(4)] + [f"R1B{j}" for j in range(4)] + ["R2A", "R2B"]:
+    for group in [f"R1A{j}" for j in range(4)] + [f"R1B{j}" for j in range(4)] + [f"R2A{j}" for j in range(PIECES)] + [f"R2B{j}" for j in range(PIECES)]:
         names += [(group, kind) for kind in ("f1", "f3", "m1", "m3")]
-    names += [("pipe", "A"), ("pipe", "B")]
+    names += [("pipe", f"{half}{j}") for half in "AB" for j in range(PIECES)]
     return {name: index for index, name in enumerate(names)}
 
 
@@ -43,7 +44,7 @@
 def kernel(
     inbox, gain, w_hbm, short_w, long_h, skip, wo_hbm, out,
     x, w, acc, wo, gated, land_fa, land_fb, land_ma, land_mb, land2_fa, land2_fb, land2_ma, land2_mb,
-    win, win3, taps, send_sem, recv_sem, load_sem,
+    win, win3, taps, tails, send_sem, recv_sem, load_sem,
 ):
     p = lax.axis_index("pipe")
     m = lax.axis_index("mp")
@@ -106,15 +107,34 @@
             self.msg("n3", 3, FULL, self.to3).wait_recv()
             self.msg("v1", 3, BOTTOM, self.to1).start()
 
+        def arrive(self):
+            self.msg("n1", 1, FULL, self.to1).wait_recv()
+            self.msg("n3", 3, FULL, self.to3).wait_recv()
+
+        def pass1(self):
+            self.msg("v3", 1, TOP, self.to3).start()
+
+        def pass3(self):
+            self.msg("v1", 3, BOTTOM, self.to1).start()
+
         def far(self):
             self.msg("v3", 2, TOP, self.to3).wait_recv()
             self.msg("v1", 2, BOTTOM, self.to1).wait_recv()
 
-        def sent(self):
+        def sent_direct(self):
             self.msg("n1", 0, FULL, self.to1).wait_send()
             self.msg("n3", 0, FULL, self.to3).wait_send()
+
+        def sent_forward1(self):
             self.msg("v3", 1, TOP, self.to3).wait_send()
+
+        def sent_forward3(self):
             self.msg("v1", 3, BOTTOM, self.to1).wait_send()
+
+        def sent(self):
+            self.sent_direct()
+            self.sent_forward1()
+            self.sent_forward3()
 
     class Reduce(Ring):
         def __init__(self, group, dim, other, cols, far, near):
@@ -177,8 +197,14 @@
     reduce_a, reduce_b = (0, REDUCE_A), (REDUCE_A, DW - REDUCE_A)
     r1a = [Reduce(f"R1A{j}", "z", ys[j], reduce_a, land_fa.at[j], land_ma.at[j]) for j in range(4)]
     r1b = [Reduce(f"R1B{j}", "y", zs[j], reduce_b, land_fb.at[j], land_mb.at[j]) for j in range(4)]
-    r2a = Reduce("R2A", "y", z, reduce_a, land2_fa, land2_ma)
-    r2b = Reduce("R2B", "z", y, reduce_b, land2_fb, land2_mb)
+    cut_a, cut_b = reduce_a[1] // PIECES, reduce_b[1] // PIECES
+    r2a = [
+        Reduce(f"R2A{j}", "y", z, (cut_a * j, cut_a), land2_fa.at[j], land2_ma.at[j]) for j in range(PIECES)
+    ]
+    r2b = [
+        Reduce(f"R2B{j}", "z", y, (REDUCE_A + cut_b * j, cut_b), land2_fb.at[j], land2_mb.at[j])
+        for j in range(PIECES)
+    ]
 
     def normalize(r, carry):
         rows = pl.ds(pl.multiple_of(r * 16, 16), 16)
@@ -195,38 +221,48 @@
         acc[first + zz] += part[:ROWS]
         acc[first + SIDE + zz] += part[ROWS:]
 
-    def project_b(yy):
-        def two(k, carry):
-            lo = yy * SIDE + 2 * k
-            left = x[pl.ds(lo, 2), :, pl.ds(*gather_b)].reshape(2 * ROWS, gather_b[1])
-            part = jnp.dot(left, w[pl.ds(*gather_b), :], preferred_element_type=F32)
-            acc[lo] += part[:ROWS]
-            acc[lo + 1] += part[ROWS:]
+    def project_columns(*columns):
+        for first, zz in columns:
+            project_a(first, zz)
+
+    def project_b(yy, pair):
+        lo = yy * SIDE + 2 * pair
+        left = x[pl.ds(lo, 2), :, pl.ds(*gather_b)].reshape(2 * ROWS, gather_b[1])
+        part = jnp.dot(left, w[pl.ds(*gather_b), :], preferred_element_type=F32)
+        acc[lo] += part[:ROWS]
+        acc[lo + 1] += part[ROWS:]
+
+    def project_row(yy):
+        lax.fori_loop(0, 2, lambda pair, c: (project_b(yy, pair), c)[1], 0)
+
+    def keep_tails(first):
+        def step(k, carry):
+            tails[first + k] = acc[first + k, pl.ds(ROWS - 8, 8), :].astype(BF16).astype(F32)
             return carry
 
-        lax.fori_loop(0, 2, two, 0)
-
-    def short_filter(first):
+        lax.fori_loop(0, SEQ_CHUNKS, step, 0)
+
+    def short_filter(first, start, stop):
         def step(k, carry):
-            i = SEQ_CHUNKS - 1 - k // 3
+            i = k // 3
             lane = pl.multiple_of((k % 3) * LANES, LANES)
             chunk = first + i
             prev = jnp.maximum(chunk - 1, first)
             streams = []
             for s in range(3):
                 cols = pl.ds(s * CHANS + lane, LANES)
-                head = acc[prev, pl.ds(ROWS - 8, 8), cols].astype(BF16).astype(F32)
+                head = tails[prev, :, cols]
                 win3[s, pl.ds(0, 8), :] = jnp.where(i > 0, head, jnp.zeros_like(head))
                 win3[s, pl.ds(8, ROWS), :] = acc[chunk, :, cols].astype(BF16).astype(F32)
-                value = short_w[pl.ds(0, 1), cols] * win3[s, pl.ds(8, ROWS), :]
+                value = short_w[s, :, pl.ds(lane, LANES)] * win3[s, pl.ds(8, ROWS), :]
                 for j in range(1, KSHORT):
-                    value = value + short_w[pl.ds(j, 1), cols] * win3[s, pl.ds(8 - j, ROWS), :]
+                    value = value + short_w[3 * j + s, :, pl.ds(lane, LANES)] * win3[s, pl.ds(8 - j, ROWS), :]
                 streams.append(value)
             acc[chunk, :, pl.ds(lane, LANES)] = streams[0]
             acc[chunk, :, pl.ds(CHANS + lane, LANES)] = (streams[1] * streams[2]).astype(BF16).astype(F32)
             return carry
 
-        lax.fori_loop(0, SEQ_CHUNKS * 3, step, 0)
+        lax.fori_loop(start * 3, stop * 3, step, 0)
 
     def long_filter(first, start, count):
         def step(k, carry):
@@ -251,18 +287,14 @@
 
         lax.fori_loop(0, count * 3, step, 0)
 
-    def mix(yy, pair):
-        lo = yy * SIDE + 2 * pair
-        left = gated[pl.ds(lo, 2)].reshape(2 * ROWS, CHANS)
-
-        def tile(n, carry):
-            cols = pl.ds(pl.multiple_of(n * 1024, 1024), 1024)
-            part = jnp.dot(left, wo[:, cols], preferred_element_type=F32).astype(BF16)
-            x[lo, :, cols] = part[:ROWS]
-            x[lo + 1, :, cols] = part[ROWS:]
-            return carry
-
-        lax.fori_loop(0, DW // 1024, tile, 0)
+    def mix(yy, first, count, cols):
+        lo = yy * SIDE + first
+        left = gated[pl.ds(lo, count)].reshape(count * ROWS, CHANS)
+        for start in range(cols[0], cols[0] + cols[1], 1024):
+            tile = pl.ds(start, min(1024, cols[0] + cols[1] - start))
+            part = jnp.dot(left, wo[:, tile], preferred_element_type=F32).astype(BF16)
+            for k in range(count):
+                x[lo + k, :, tile] = part[k * ROWS : (k + 1) * ROWS]
 
     lax.fori_loop(0, ROWS // 16, normalize, 0)
     pl.semaphore_wait(barrier, len(neighbours))
@@ -283,112 +315,172 @@
     own = (y // 2) * SEQ_CHUNKS
     other = (1 - y // 2) * SEQ_CHUNKS
 
+    far_pair, near_pair = 1 - z // 2, z // 2
+
+    def start_of(row, first):
+        return row * SIDE - first
+
+    from2 = start_of(ys[2], other)
+    lo = from2 + 2 * far_pair
+    need = jnp.maximum(lo - 1, 0)
+    hands = []
+
+    def finish(half, k, ring):
+        ring.total(inbox)
+        hand = message(("pipe", f"{half}{k}"), ring.at(0, FULL), out.at[:, pl.ds(*ring.cols)], (after, m))
+        hand.start()
+        hands.append(hand)
+
+    g1b.forward1()
     g1a.forward1()
-    g2a[1].send()
     g1a.forward3()
-    g1b.forward1()
-    g2b[1].send()
     g1b.forward3()
     g2b[3].send()
     g2a[0].forward1()
+    g2a[1].send()
+    g1b.far()
+    g2a[3].send()
+    g1a.far()
+    g2b[1].send()
+    project_row(y)
+    project_a(other, z)
+    g2b[2].send()
+    g2a[1].forward3()
     g2a[0].forward3()
-    g1b.far()
-    g2b[2].send()
-    project_b(y)
     g2a[1].forward1()
-    g2a[1].forward3()
-    g1a.far()
+    g2b[0].forward3()
     g2a[2].send()
-    g2a[3].send()
+    project_a(own, zs[1])
+    g2b[1].forward3()
+    g2b[1].forward1()
+    project_a(own, zs[3])
     g2b[0].forward1()
-    g2b[0].forward3()
-    project_a(other, z)
-    g2b[1].forward1()
-    g2b[1].forward3()
     g2a[0].far()
+    project_a(own, z)
+    g2a[3].forward3()
     g2a[1].far()
-    lax.fori_loop(0, SIDE, lambda zz, c: (project_a(own, zz), c)[1], 0)
+    project_b(ys[3], near_pair)
+    project_b(ys[1], near_pair)
     g2b[3].forward1()
     g2b[3].forward3()
+    project_a(own, zs[2])
+    g2a[3].forward1()
+    g2b[2].forward1()
+    g2b[2].forward3()
+    project_b(ys[1], far_pair)
+    for ring in [g1a] + g2b:
+        ring.sent_direct()
+    g1b.sent()
+    g2a[0].sent()
+    keep_tails(own)
+    short_filter(own, 0, SEQ_CHUNKS)
     g2a[2].forward1()
     g2a[2].forward3()
-    g2b[2].forward1()
-    g2b[2].forward3()
-    project_b(ys[1])
-    short_filter(own)
-    long_filter(own, 0, 4)
-    g2a[3].forward1()
-    g2a[3].forward3()
-    long_filter(own, 4, 4)
-    project_b(ys[3])
+    long_filter(own, start_of(y, own) + 2 * far_pair, 2)
+    mix(y, 2 * far_pair, 2, reduce_a)
+    r1a[0].send_far()
+    g2a[3].far()
+    long_filter(own, start_of(y, own) + 2 * near_pair, 2)
     project_a(other, zs[1])
+    g2b[0].far()
+    mix(y, 2 * near_pair, 2, reduce_a)
+    g2b[1].far()
+    long_filter(own, start_of(ys[1], own) + 2 * far_pair, 2)
+    project_b(ys[2], near_pair)
+    r1a[0].merge3()
+    g2a[2].far()
+    r1a[0].merge1()
     project_a(other, zs[3])
-    for ring in [g2a[2], g2a[3]] + g2b:
-        ring.far()
-    for ring in [g1a, g1b] + g2a + g2b:
+    project_a(other, zs[2])
+    project_b(ys[3], far_pair)
+    g2a[1].sent()
+    g2b[2].sent_forward1()
+    g2b[3].sent_forward1()
+    g2b[3].far()
+    mix(ys[1], 2 * far_pair, 2, reduce_a)
+    mix(ys[1], 2 * far_pair, 2, reduce_b)
+    g2b[2].far()
+    project_b(ys[2], far_pair)
+    keep_tails(other)
+    short_filter(other, need, lo + 2)
+    r1a[1].send_far()
+    for ring in g2a[2:]:
         ring.sent()
-
-    far_pair, near_pair = 1 - z // 2, z // 2
-    mix(y, far_pair)
-    r1a[0].send_far()
-    mix(ys[1], far_pair)
-    r1a[1].send_far()
-    project_a(other, zs[2])
-    project_b(ys[2])
-    mix(y, near_pair)
-    mix(ys[1], near_pair)
-    r1a[0].merge()
-    r1a[1].merge()
-    short_filter(other)
-    y2_at, y3_at = ys[2] * SIDE - other, ys[3] * SIDE - other
-    long_filter(other, y2_at + 2 * far_pair, 2)
-    mix(ys[2], far_pair)
+    g1a.sent_forward3()
+    for ring in g2b:
+        ring.sent_forward3()
+    long_filter(other, from2 + zs[3], 1)
+    mix(ys[2], zs[3], 1, reduce_b)
+    r1b[3].send_far()
+    long_filter(other, from2 + zs[2], 1)
+    mix(ys[2], zs[2], 1, reduce_b)
     r1b[2].send_far()
-    r1b[3].send_far()
+    g1a.sent_forward1()
+    g2b[0].sent_forward1()
+    g2b[1].sent_forward1()
+    mix(ys[2], 2 * far_pair, 2, reduce_a)
+    short_filter(other, 0, need)
+    short_filter(other, lo + 2, SEQ_CHUNKS)
+    long_filter(other, start_of(ys[3], other) + 2 * far_pair, 2)
+    mix(ys[3], 2 * far_pair, 2, reduce_b)
     r1a[2].send_far()
-    long_filter(other, y3_at + 2 * far_pair, 2)
-    mix(ys[3], far_pair)
+    r1b[3].merge1()
+    r1b[3].merge3()
+    mix(ys[3], 2 * far_pair, 2, reduce_a)
+    long_filter(other, start_of(ys[2], other) + 2 * near_pair, 2)
     r1a[3].send_far()
-    long_filter(other, y2_at + 2 * near_pair, 2)
-    mix(ys[2], near_pair)
+    mix(y, 2 * far_pair, 2, reduce_b)
+    mix(ys[2], 2 * near_pair, 2, reduce_b)
+    r1a[2].merge3()
     r1b[1].send_far()
+    r1b[2].merge3()
+    mix(ys[2], 2 * near_pair, 2, reduce_a)
+    r1a[2].merge1()
+    r1b[2].merge1()
+    long_filter(own, start_of(ys[1], own) + 2 * near_pair, 2)
+    long_filter(other, start_of(ys[3], other) + 2 * near_pair, 2)
+    mix(ys[1], 2 * near_pair, 2, reduce_b)
+    mix(ys[3], 2 * near_pair, 2, reduce_a)
+    mix(ys[3], 2 * near_pair, 2, reduce_b)
+    mix(ys[1], 2 * near_pair, 2, reduce_a)
+    mix(y, 2 * near_pair, 2, reduce_b)
+    r1a[1].merge3()
+    r1b[1].merge1()
+    r1b[1].merge3()
+    r1a[1].merge1()
     r1b[0].send_far()
-    r1b[2].merge()
-    r1b[3].merge()
-    long_filter(other, y3_at + 2 * near_pair, 2)
-    mix(ys[3], near_pair)
-    r1a[2].merge()
-    r1a[3].merge()
-    r1b[1].merge()
-    r1b[0].merge()
-    r1a[0].total()
-    r1a[1].total()
+    r1a[3].merge3()
     r1b[2].total()
-    r2b.send_far()
+    r1a[3].merge1()
     r1b[3].total()
     r1a[2].total()
-    r2a.send_far()
+    for ring in r2b:
+        ring.send_far()
+    for ring in r2a:
+        ring.send_far()
+    r1a[1].total()
+    r1b[0].merge3()
+    r1b[0].merge1()
+    r2a[0].merge1()
     r1a[3].total()
-    r2b.merge3()
     r1b[1].total()
-    r2b.merge1()
-    r2a.merge1()
-    r2a.merge3()
+    r2a[1].merge1()
+    r2b[0].merge1()
+    r2b[0].merge3()
+    r2a[0].merge3()
     r1b[0].total()
-    r2b.total(inbox)
-    hand_b = message(
-        ("pipe", "B"), region(y, z, FULL, reduce_b), out.at[:, pl.ds(*reduce_b)], (after, m)
-    )
-    hand_b.start()
-    r2a.total(inbox)
-    hand_a = message(
-        ("pipe", "A"), region(y, z, FULL, reduce_a), out.at[:, pl.ds(*reduce_a)], (after, m)
-    )
-    hand_a.start()
-    for ring in r1a + r1b + [r2a, r2b]:
+    r2b[1].merge3()
+    r2a[1].merge3()
+    r2b[1].merge1()
+    finish("B", 0, r2b[0])
+    r1a[0].total()
+    finish("A", 0, r2a[0])
+    finish("B", 1, r2b[1])
+    finish("A", 1, r2a[1])
+    for ring in r1a + r1b + r2a + r2b:
         ring.sent()
-    hand_a.wait()
-    hand_b.wait()
+    for hand in hands:
+        hand.wait()
 
 
 def on_device(inbox, norm_gain, w_in, short_w, long_h, skip_gain, w_out):
@@ -411,13 +503,14 @@
             pltpu.VMEM((4, 2, ROWS // 2, wide_b), BF16),
             pltpu.VMEM((4, 2, ROWS, wide_a), BF16),
             pltpu.VMEM((4, 2, ROWS, wide_b), BF16),
-            pltpu.VMEM((2, ROWS // 2, wide_a), BF16),
-            pltpu.VMEM((2, ROWS // 2, wide_b), BF16),
-            pltpu.VMEM((2, ROWS, wide_a), BF16),
-            pltpu.VMEM((2, ROWS, wide_b), BF16),
+            pltpu.VMEM((PIECES, 2, ROWS // 2, wide_a // PIECES), BF16),
+            pltpu.VMEM((PIECES, 2, ROWS // 2, wide_b // PIECES), BF16),
+            pltpu.VMEM((PIECES, 2, ROWS, wide_a // PIECES), BF16),
+            pltpu.VMEM((PIECES, 2, ROWS, wide_b // PIECES), BF16),
             pltpu.VMEM((2 * ROWS, LANES), F32),
             pltpu.VMEM((3, ROWS + 8, LANES), F32),
             pltpu.VMEM((FILT, CHANS), F32),
+            pltpu.VMEM((SIDE * SIDE, 8, 3 * CHANS), F32),
             pltpu.SemaphoreType.DMA((count,)),
             pltpu.SemaphoreType.DMA((count,)),
             pltpu.SemaphoreType.DMA((4,)),
@@ -431,7 +524,7 @@
         inbox[0],
         norm_gain,
         jnp.transpose(w_in[0], (1, 0, 2)),
-        short_w[0].reshape(KSHORT, 3 * CHANS),
+        short_w[0].reshape(KSHORT * 3, 1, CHANS),
         long_h[0],
         skip_gain,
         w_out[0],

time: 215 us -> 194 us (0.902)
  Pallas kernels: 210 us -> 191 us
    pallas_call x1, Pallas kernels: 210 us -> 191 us  [on_device(): pl.pallas_call(kernel, out_shape=jax.ShapeDtypeStruct((ROWS, DW), BF16),...]
where the time goes in v2:
time: 194 us
  Pallas kernels  191 us (98%)
  local copies, waits for them, and re-layouts  2.29 us (1%)
    pallas_call x1, Pallas kernels, on_device(): pl.pallas_call(kernel, out_shape=jax.ShapeDtypeStruct((ROWS, DW), BF16),...  191 us

profile of v2, /device:TPU:0, one launch (start us, length us, event | category | flops | bytes accessed | tf_op | source)
XLA Modules:
  0.0 193.7 jit_solution(8796177459342474163)
XLA Ops:
  0.0 191.5 %relay_block.1 = bf16[128,4096]{1,0:T(8,128)(2,1)} custom-call(bf16[128,4096]{1,0:T(8,128)(2,1)} %bitcast.11, f32[1,4096]{1,0:T(1,128)} %gain.1, bf16[3,4096,384]{2,1,0:T(8,128)(2,1)} %bitcast.9, f32[21,1,384]{2,1,0:T(1,128)} %bitcast.13, bf16[128,384]{1,0:T(8,128)(2,1)} %bitcast.12, f32[1,384]{1,0:T(1,128)} %skip.1, bf16[384,4096]{1,0:T(8,128)(2,1)} %bitcast.10), custom_call_target="tpu_custom_call" | custom-call | flops 27000000512 | bytes 20000000 | tf_op jit(solution)/shard_map/relay_block/pallas_call | solution.py:491
  191.5 2.3 %copy.9 = bf16[1,128,4096]{2,1,0:T(8,128)(2,1)} copy(bf16[1,128,4096]{2,1,0:T(8,128)(2,1)} %bitcast.8) | data formatting | bytes 2097152
